TPU v7x, 128 devices: a whole 4x4x4 slice. The times are simulated.
128 devices in a mesh: morton: 32 (over z, y, core), lane: 4 (over x).
Axes of the slice: x: 4, y: 4, z: 4, core: 2. Of those that a mesh axis runs over, the one named last changes fastest.
Arguments:
- cons_old: float32 [4096, 8, 4096], P(('morton', 'lane')), may hold values from -6 to 6
- flagged: int32 [256], replicated, may hold values from 0 to 4095, as said below
- new_owner: int32 [256], replicated, may hold values from 0 to 127, as said below
- diffusivity: float32 [8], replicated, may hold values from 0.02 to 0.1
- courant: float32 [8], replicated, may hold values from 0.05 to 0.3
Outputs:
- coarse_next: float32 [4096, 8, 4096], P(('morton', 'lane'))
- children: float32 [384, 8, 8, 4096], P(('morton', 'lane'))
Inputs may be any that keep to these rules, and one draw needn't show every extreme that they name: `flagged`: Strictly increasing. The 32 meshblocks of one device hold 0 to 4 flagged parents, some device exactly 4. `new_owner`: Nondecreasing. Each device receives the children of 1 to 3 parents, some device exactly 3. A parent's new owner differs from the device that holds it (flagged // 32) by at most 2, and by exactly 2 in either direction for some parent.
All inputs are finite; a program needn't handle non-finite values.
Results may differ from a plain program's by a relative error of at most 0.000052.
Values sent between devices are 32-bit elements; how exact they have to be, the bound alone decides.
No kernel may reach another device: no remote copies, remote signals or barrier semaphores. Data moves between devices by JAX's collectives and lax.ppermute only.
A program may use at most 192 MiB of HBM per device.

v0:
```python
import jax
import jax.numpy as jnp
from jax import lax
from jax.sharding import PartitionSpec as P

EDGE = 16
PAR_DEV = 2


def extended(block, sides, width):
    for axis, dim in sides:
        count = lax.axis_size(axis)
        forward = [(i, i + 1) for i in range(count - 1)]
        backward = [(target, source) for source, target in forward]
        low = lax.ppermute(
            lax.slice_in_dim(block, block.shape[dim] - width, None, axis=dim), axis, forward
        )
        high = lax.ppermute(lax.slice_in_dim(block, 0, width, axis=dim), axis, backward)
        block = jnp.concatenate([low, block, high], axis=dim)
    return block


def from_behind(value, axis, steps):
    count = lax.axis_size(axis)
    first, last = (max(0, -steps), min(count, count - steps))
    return lax.ppermute(value, axis, [(source, source + steps) for source in range(first, last)])


def prolong_tables(extent):
    last = extent - 1
    rows = jnp.arange(extent, dtype=jnp.int32)
    lower = jnp.clip(rows - 1, 0, last)
    upper = jnp.clip(rows + 1, 0, last)
    width = (upper - lower).astype(jnp.float32)
    cols = jnp.arange(extent, dtype=jnp.int32)
    slopes = (
        (cols[None, :] == upper[:, None]).astype(jnp.float32)
        - (cols[None, :] == lower[:, None]).astype(jnp.float32)
    ) / width[:, None]
    ident = (cols[None, :] == rows[:, None]).astype(jnp.float32)
    even = ident - 0.25 * slopes
    odd = ident + 0.25 * slopes
    refine_op = jnp.stack([even, odd], 1).reshape(2 * extent, extent)
    halves = refine_op.reshape(2, extent, extent)
    crossed = jnp.einsum(
        "ybj,zck->jkyzbc", halves, halves, precision=lax.Precision.HIGHEST
    ).reshape(extent * extent, 4 * extent * extent)
    return (halves, crossed)


def prolong(parents, halves, crossed):
    number, fields, volume = parents.shape
    extent = halves.shape[1]
    rows_flat = parents.reshape(number * fields * extent, extent * extent)
    planes = jnp.dot(
        rows_flat, crossed, precision=lax.Precision.HIGHEST, preferred_element_type=jnp.float32
    )
    planes = planes.reshape(number, fields, extent, 4, extent * extent)
    result = jnp.einsum("xai,nfiqc->nxqfac", halves, planes, precision=lax.Precision.HIGHEST)
    return result.reshape(number, 8, fields, volume)


def gather_blocks(message_data, dispatch_blocks, block_offsets, transfer_buffer):
    parent_max = message_data.shape[0]
    incoming_blocks = []
    for step_spacing in (-2, -1, 0, 1, 2):
        selected = dispatch_blocks & (block_offsets == step_spacing)
        shaped = selected.reshape((parent_max,) + (1,) * (message_data.ndim - 1))
        departing_blocks = jnp.where(shaped, message_data, jnp.float32(0.0))
        if step_spacing == 0:
            incoming_blocks.append(departing_blocks)
        else:
            incoming_blocks.append(transfer_buffer(departing_blocks, step_spacing))
    return jnp.concatenate(incoming_blocks, 0)


def shards(cons_old, flagged, new_owner, diffusivity, courant):
    own_blocks, fields, volume = cons_old.shape
    extent = EDGE
    plane_len = extent * extent
    grid = cons_old.reshape(own_blocks, fields, extent, plane_len)
    rim_pair = jnp.stack([grid[0, :, 0], grid[-1, :, -1]], 0)
    framed = extended(rim_pair, ((("morton", "lane"), 0),), 1)
    last_planes = jnp.concatenate([framed[0][None], grid[:-1, :, -1]], 0)
    first_planes = jnp.concatenate([grid[1:, :, 0], framed[3][None]], 0)
    behind = jnp.concatenate([last_planes[:, :, None], grid[:, :, :-1]], 2)
    forward = jnp.concatenate([grid[:, :, 1:], first_planes[:, :, None]], 2)
    zpos = jnp.arange(plane_len, dtype=jnp.int32) % extent
    zplus = jnp.where(zpos == extent - 1, jnp.roll(grid, extent - 1, -1), jnp.roll(grid, -1, -1))
    zminus = jnp.where(zpos == 0, jnp.roll(grid, -(extent - 1), -1), jnp.roll(grid, 1, -1))
    beside_all = (
        behind + forward + jnp.roll(grid, extent, -1) + jnp.roll(grid, -extent, -1) + zplus + zminus
    )
    diffuse = diffusivity[None, :, None, None]
    advect = courant[None, :, None, None]
    stepped = grid + diffuse * (beside_all - 6.0 * grid) - advect * (grid - behind)
    coarse_next = stepped.reshape(own_blocks, fields, volume)
    myself = lax.axis_index(("morton", "lane"))
    parent_max = 2 * PAR_DEV
    capacity = PAR_DEV + 1
    parent_total = flagged.shape[0]
    mine_first = jnp.sum((flagged < myself * own_blocks).astype(jnp.int32))
    rank_ids = mine_first + jnp.arange(parent_max, dtype=jnp.int32)
    picked = jnp.minimum(rank_ids, parent_total - 1)
    dispatch_blocks = (rank_ids < parent_total) & (flagged[picked] // own_blocks == myself)
    local_idx = jnp.clip(flagged[picked] - myself * own_blocks, 0, own_blocks - 1)
    parents = jnp.take(cons_old, local_idx, axis=0)
    block_offsets = new_owner[picked] - myself
    first_new = jnp.sum((new_owner < myself).astype(jnp.int32))
    wanted = first_new + jnp.arange(capacity, dtype=jnp.int32)
    chosen = jnp.minimum(wanted, parent_total - 1)
    keeping = (wanted < parent_total) & (new_owner[chosen] == myself)
    source = flagged[chosen] // own_blocks
    source_first = jnp.sum(
        (flagged[None, :] < (source * own_blocks)[:, None]).astype(jnp.int32), axis=1
    )
    row_index = (myself - source + 2) * parent_max + (chosen - source_first)
    row_index = jnp.clip(row_index, 0, 5 * parent_max - 1)
    halves, crossed = prolong_tables(extent)
    message_data = prolong(parents, halves, crossed)

    def transfer_buffer(departing_blocks, step_spacing):
        return from_behind(departing_blocks, ("morton", "lane"), step_spacing)

    combined_blocks = gather_blocks(message_data, dispatch_blocks, block_offsets, transfer_buffer)
    arrived = jnp.take(combined_blocks, row_index, axis=0)
    children = jnp.where(keeping[:, None, None, None], arrived, jnp.float32(0.0))
    return (coarse_next, children)


def solution(mesh):
    in_specs = (P(("morton", "lane"), None, None), P(), P(), P(), P())
    out_specs = (P(("morton", "lane"), None, None), P(("morton", "lane"), None, None, None))
    return jax.shard_map(shards, mesh=mesh, in_specs=in_specs, out_specs=out_specs, check_vma=False)
```

profile of v0, /device:TPU:96, one launch (start us, length us, event | category | flops | bytes accessed | tf_op | source)
XLA Modules:
  0.0 441.2 jit_solution(5696784350392576640)
XLA Ops:
  0.7 1.3 fusion.9
  2.7 1.3 gather_fusion.2
  4.0 1.3 gather_fusion.3
  5.3 0.7 compare_and_fusion
  6.2 4.4 %multiply_bitcast_fusion = f32[16,16,2,2,16,16]{5,4,3,2,1,0:T(8,128)} fusion(f32[2,16,16]{1,0,2:T(2,128)S(1)} %copy.16), kind=kLoop, calls=%fused_computation.6 | loop fusion | flops 262144 | bytes 1050624 | tf_op jit(solution)/shard_map/ybj,zck->jkyzbc/transpose | solution.py:45
  10.6 7.9 %reshape.468 = f32[256,1024]{1,0:T(8,128)S(1)} reshape(f32[16,16,2,2,16,16]{5,4,3,2,1,0:T(8,128)} %multiply_bitcast_fusion) | data formatting | bytes 2097152 | tf_op jit(solution)/shard_map/reshape | solution.py:47
  18.8 2.8 gather_fusion.4
  21.7 2.0 fusion.1
  23.7 3.4 convolution_bitcast_fusion
  27.1 2.7 copy.20
  29.8 5.0 %reshape.469 = f32[4,8,8,4096]{3,2,1,0:T(8,128)} reshape(f32[4,2,4,8,16,256]{5,4,3,2,1,0:T(8,128)} %copy.20) | data formatting | bytes 8388608 | tf_op jit(solution)/shard_map/reshape | solution.py:60
  34.8 6.5 %broadcast_select_fusion.2 = (f32[4,8,8,4096]{3,2,1,0:T(8,128)}, f32[4,8,8,4096]{3,2,1,0:T(8,128)}) fusion(f32[4,8,8,4096]{3,2,1,0:T(8,128)} %reshape.469, pred[4]{0:T(512)(128)(4,1)S(1)} %get-tuple-element.34, pred[4]{0:T(512)(128)(4,1)S(1)} %get-tuple-element.35), kind=kLoop, calls=%fused_computation.22 | loop fusion | flops 2097152 | bytes 12582920 | tf_op jit(solution)/shard_map/jit(_where)/select_n | solution.py:69
  41.4 6.6 %collective-permute-start.2 = (f32[4,8,8,4096]{3,2,1,0:T(8,128)}, f32[4,8,8,4096]{3,2,1,0:T(8,128)}, u32[]{:S(2)}, u32[]{:S(2)}) collective-permute-start(f32[4,8,8,4096]{3,2,1,0:T(8,128)} %get-tuple-element.11), channel_id=1, source_target_pairs={{2,0},{3,1},{4,2},{5,3},{6,4},{7,5},{8,6},{9,7},{10,8},{11,9},{12,... | collective-permute-start | bytes 12582920 | tf_op jit(solution)/shard_map/ppermute | solution.py:26
  48.0 2.8 collective-permute-start.3
  50.8 0.7 slice_bitcast_fusion.2
  51.5 3.1 collective-permute-start
  54.6 6.9 %collective-permute-start.1 = (f32[1,8,256]{2,1,0:T(8,128)S(1)}, f32[1,8,256]{2,1,0:T(8,128)S(1)}, u32[]{:S(2)}, u32[]{:S(2)}) collective-permute-start(f32[1,8,256]{2,1,0:T(8,128)S(1)} %get-tuple-element.16), channel_id=1, source_target_pairs={{1,0},{2,1},{3,2},{4,3},{5,4},{6,5},{7,6},{8,7},{9,8},{10,9},{11,1... | collective-permute-start | bytes 24584 | tf_op jit(solution)/shard_map/ppermute | solution.py:18
  64.3 0.7 fusion.13
  65.0 0.7 compare_and_fusion.7
  65.6 1.1 slice_bitcast_fusion
  66.8 5.1 %fusion.17 = (f32[32,8,16,16]{3,1,2,0:T(8,128)}, f32[32,8,16,16]{3,1,2,0:T(8,128)}) fusion(f32[32,8,16,256]{3,1,2,0:T(8,128)} %bitcast.86), kind=kLoop, calls=%fused_computation.102 | loop fusion | bytes 1048576 | tf_op jit(solution)/shard_map/jit(_roll_static)/slice | solution.py:92
  71.8 3.6 fusion.18
  75.4 8.9 %pad_maximum_fusion.2 = (f32[32,8,16,256]{3,1,2,0:T(8,128)}, f32[32,8,16,256]{3,1,2,0:T(8,128)}) fusion(f32[32,8,16,240]{3,1,2,0:T(8,128)S(1)} %get-tuple-element.20, f32[32,8,16,16]{3,1,2,0:T(8,128)} %get-tuple-element.18, f32[32,8,16,16]{3,1,2,0:T(8,128)} %get-tuple-element.19, f32[32,8,16,240]{3,1,2,0:T(8,128)} %get-tuple-element.21), kind=kLoop, calls=%fused_computation.9 | loop fusion | flops 2097152 | bytes 16777216 | tf_op jit(solution)/shard_map/jit(_roll_static)/concatenate | solution.py:92
  84.3 2.8 fusion.21
  87.1 3.6 fusion.22
  90.7 9.0 %pad_maximum_fusion.4 = (f32[32,8,16,256]{3,1,2,0:T(8,128)}, f32[32,8,16,256]{3,1,2,0:T(8,128)}) fusion(f32[32,8,16,241]{3,1,2,0:T(8,128)S(1)} %get-tuple-element.28, f32[32,8,16,15]{3,1,2,0:T(8,128)} %get-tuple-element.26, f32[32,8,16,15]{3,1,2,0:T(8,128)} %get-tuple-element.27, f32[32,8,16,241]{3,1,2,0:T(8,128)} %get-tuple-element.29), kind=kLoop, calls=%fused_computation.11 | loop fusion | flops 2097152 | bytes 16777216 | tf_op jit(solution)/shard_map/jit(_roll_static)/concatenate | solution.py:89
  99.7 2.8 fusion.20
  102.4 35.1 %collective-permute-done.2 = f32[4,8,8,4096]{3,2,1,0:T(8,128)} collective-permute-done((f32[4,8,8,4096]{3,2,1,0:T(8,128)}, f32[4,8,8,4096]{3,2,1,0:T(8,128)}, u32[]{:S(2)}, u32[]{:S(2)}) %collective-permute-start.2) | collective-permute-done | bytes 4194336 | tf_op jit(solution)/shard_map/ppermute | solution.py:26
  137.5 4.6 %constant_dynamic-update-slice_fusion.3 = f32[20,8,8,4096]{3,2,1,0:T(8,128)} fusion(f32[4,8,8,4096]{3,2,1,0:T(8,128)} %collective-permute-done.2), kind=kLoop, calls=%fused_computation.38 | loop fusion | bytes 8388608
  142.1 85.9 %collective-permute-done.3 = f32[4,8,8,4096]{3,2,1,0:T(8,128)} collective-permute-done((f32[4,8,8,4096]{3,2,1,0:T(8,128)}, f32[4,8,8,4096]{3,2,1,0:T(8,128)}, u32[]{:S(2)}, u32[]{:S(2)}) %collective-permute-start.3) | collective-permute-done | bytes 4194336 | tf_op jit(solution)/shard_map/ppermute | solution.py:26
  228.1 4.7 %constant_dynamic-update-slice_fusion.2 = f32[20,8,8,4096]{3,2,1,0:T(8,128)} fusion(f32[20,8,8,4096]{3,2,1,0:T(8,128)} %constant_dynamic-update-slice_fusion.3, f32[4,8,8,4096]{3,2,1,0:T(8,128)} %collective-permute-done.3), kind=kLoop, calls=%fused_computation.37 | loop fusion | bytes 8388608
  232.7 5.0 %broadcast_select_fusion = (f32[4,8,8,4096]{3,2,1,0:T(8,128)}, f32[4,8,8,4096]{3,2,1,0:T(8,128)}, f32[20,8,8,4096]{3,2,1,0:T(8,128)}) fusion(f32[4,8,8,4096]{3,2,1,0:T(8,128)S(1)} %copy-done.4, pred[4]{0:T(512)(128)(4,1)S(1)} %get-tuple-element.4, pred[4]{0:T(512)(128)(4,1)S(1)} %get-tuple-element.32, ...), kind=kLoop, calls=%fused_computation.20 | loop fusion | flops 3145728 | bytes 16777228 | tf_op jit(solution)/shard_map/jit(_where)/select_n | solution.py:69
  237.7 2.7 collective-permute-start.4
  240.4 3.5 fusion.19
  244.0 5.2 %collective-permute-start.5 = (f32[4,8,8,4096]{3,2,1,0:T(8,128)}, f32[4,8,8,4096]{3,2,1,0:T(8,128)}, u32[]{:S(2)}, u32[]{:S(2)}) collective-permute-start(f32[4,8,8,4096]{3,2,1,0:T(8,128)} %get-tuple-element.7), channel_id=1, source_target_pairs={{0,2},{1,3},{2,4},{3,5},{4,6},{5,7},{6,8},{7,9},{8,10},{9,11},{10,... | collective-permute-start | bytes 12582920 | tf_op jit(solution)/shard_map/ppermute | solution.py:26
  249.2 8.6 %pad_maximum_fusion.5 = (f32[32,8,16,256]{3,1,2,0:T(8,128)}, f32[32,8,16,256]{3,1,2,0:T(8,128)}) fusion(f32[32,8,16,1]{3,1,2,0:T(8,128)} %get-tuple-element.24, f32[32,8,16,255]{3,1,2,0:T(8,128)S(1)} %get-tuple-element.22, f32[32,8,16,255]{3,1,2,0:T(8,128)} %get-tuple-element.23, f32[32,8,16,1]{3,1,2,0:T(8,128)} %get-tuple-element.25), kind=kLoop, calls=%fused_computation.12 | loop fusion | flops 2097152 | bytes 16777216 | tf_op jit(solution)/shard_map/jit(_roll_static)/concatenate | solution.py:89
  257.8 3.7 fusion.16
  261.7 4.9 %pad_maximum_fusion.1 = f32[32,8,16,256]{3,1,2,0:T(8,128)} fusion(f32[32,8,1,256]{3,1,2,0:T(8,128)S(1)} %get-tuple-element.38, f32[32,8,15,256]{3,1,2,0:T(8,128)} %get-tuple-element.12), kind=kLoop, calls=%fused_computation.8 | loop fusion | flops 1048576 | bytes 8388608 | tf_op jit(solution)/shard_map/concatenate | solution.py:87
  266.7 2.7 pad_maximum_fusion
  269.4 1.3 copy-done.3
  270.7 1.2 copy-done.5
  271.9 12.3 %multiply_subtract_fusion = f32[32,8,4096]{2,1,0:T(8,128)} fusion(f32[32,8,4096]{2,1,0:T(8,128)S(1)} %copy-done.3, f32[32,8,4096]{2,1,0:T(8,128)} %bitcast.100, f32[32,8,4096]{2,1,0:T(8,128)} %bitcast.96, f32[32,8,4096]{2,1,0:T(8,128)} %bitcast.98, f32[32,8,4096]{2,1,0:T(8,128)} %bitcast.95, f32[32,8,4096]{2,1,0:T(8,128)} %bitcast.97, ...), kind=kLoop, calls=%fused_computation.16 | loop fusion | flops 14680064 | bytes 41951296 | tf_op jit(solution)/shard_map/sub | solution.py:96
  284.2 52.1 %collective-permute-done.4 = f32[4,8,8,4096]{3,2,1,0:T(8,128)} collective-permute-done((f32[4,8,8,4096]{3,2,1,0:T(8,128)}, f32[4,8,8,4096]{3,2,1,0:T(8,128)}, u32[]{:S(2)}, u32[]{:S(2)}) %collective-permute-start.4) | collective-permute-done | bytes 4194336 | tf_op jit(solution)/shard_map/ppermute | solution.py:26
  336.3 4.6 %constant_dynamic-update-slice_fusion.1 = f32[20,8,8,4096]{3,2,1,0:T(8,128)} fusion(f32[20,8,8,4096]{3,2,1,0:T(8,128)} %get-tuple-element.9, f32[4,8,8,4096]{3,2,1,0:T(8,128)} %collective-permute-done.4), kind=kLoop, calls=%fused_computation.36 | loop fusion | bytes 8388608
  340.9 86.0 %collective-permute-done.5 = f32[4,8,8,4096]{3,2,1,0:T(8,128)} collective-permute-done((f32[4,8,8,4096]{3,2,1,0:T(8,128)}, f32[4,8,8,4096]{3,2,1,0:T(8,128)}, u32[]{:S(2)}, u32[]{:S(2)}) %collective-permute-start.5) | collective-permute-done | bytes 4194336 | tf_op jit(solution)/shard_map/ppermute | solution.py:26
  426.8 4.6 %constant_dynamic-update-slice_fusion = f32[20,8,8,4096]{3,2,1,0:T(8,128)} fusion(f32[20,8,8,4096]{3,2,1,0:T(8,128)} %constant_dynamic-update-slice_fusion.1, f32[4,8,8,4096]{3,2,1,0:T(8,128)} %collective-permute-done.5), kind=kLoop, calls=%fused_computation.35 | loop fusion | bytes 8388608 | tf_op jit(solution)/shard_map/concatenate | solution.py:74
  431.4 7.7 %gather_fusion.5 = f32[3,8,8,4096]{3,2,1,0:T(8,128)S(1)} fusion(f32[20,8,8,4096]{3,2,1,0:T(8,128)} %constant_dynamic-update-slice_fusion, s32[1024]{0:T(1024)S(1)} %pad_clamp_fusion), kind=kCustom, calls=%fused_computation.5 | custom fusion | bytes 6291468 | tf_op jit(solution)/shard_map/jit(_take)/gather | solution.py:126
  439.1 2.1 select_select_fusion
  (47 shorter events, 4.3 us)
Async XLA Ops:
  34.8 26.7 %copy-start.1 = (s32[256]{0:T(256)S(1)}, s32[256]{0:T(256)}, u32[]{:S(2)}) copy-start(s32[256]{0:T(256)} %param.7) | copy-start | bytes 3076
  34.8 28.0 %copy-start = (s32[256]{0:T(256)S(1)}, s32[256]{0:T(256)}, u32[]{:S(2)}) copy-start(s32[256]{0:T(256)} %param.6) | copy-start | bytes 3076
  41.4 96.2 %collective-permute-start.2 = (f32[4,8,8,4096]{3,2,1,0:T(8,128)}, f32[4,8,8,4096]{3,2,1,0:T(8,128)}, u32[]{:S(2)}, u32[]{:S(2)}) collective-permute-start(f32[4,8,8,4096]{3,2,1,0:T(8,128)} %get-tuple-element.11), channel_id=1, source_target_pairs={{2,0},{3,1},{4,2},{5,3},{6,4},{7,5},{8,6},{9,7},{10,8},{11,9},{12,... | collective-permute-start | bytes 12582920 | tf_op jit(solution)/shard_map/ppermute | solution.py:26
  48.0 180.0 %collective-permute-start.3 = (f32[4,8,8,4096]{3,2,1,0:T(8,128)}, f32[4,8,8,4096]{3,2,1,0:T(8,128)}, u32[]{:S(2)}, u32[]{:S(2)}) collective-permute-start(f32[4,8,8,4096]{3,2,1,0:T(8,128)} %get-tuple-element.10), channel_id=1, source_target_pairs={{1,0},{2,1},{3,2},{4,3},{5,4},{6,5},{7,6},{8,7},{9,8},{10,9},{11,1... | collective-permute-start | bytes 12582920 | tf_op jit(solution)/shard_map/ppermute | solution.py:26
  51.5 210.1 %collective-permute-start = (f32[1,8,256]{2,1,0:T(8,128)S(1)}, f32[1,8,256]{2,1,0:T(8,128)S(1)}, u32[]{:S(2)}, u32[]{:S(2)}) collective-permute-start(f32[1,8,256]{2,1,0:T(8,128)S(1)} %get-tuple-element.17), channel_id=1, source_target_pairs={{0,1},{1,2},{2,3},{3,4},{4,5},{5,6},{6,7},{7,8},{8,9},{9,10},{10,1... | collective-permute-start | bytes 24584 | tf_op jit(solution)/shard_map/ppermute | solution.py:15
  54.6 207.0 %collective-permute-start.1 = (f32[1,8,256]{2,1,0:T(8,128)S(1)}, f32[1,8,256]{2,1,0:T(8,128)S(1)}, u32[]{:S(2)}, u32[]{:S(2)}) collective-permute-start(f32[1,8,256]{2,1,0:T(8,128)S(1)} %get-tuple-element.16), channel_id=1, source_target_pairs={{1,0},{2,1},{3,2},{4,3},{5,4},{6,5},{7,6},{8,7},{9,8},{10,9},{11,1... | collective-permute-start | bytes 24584 | tf_op jit(solution)/shard_map/ppermute | solution.py:18
  66.7 5.1 %copy-start.2 = (f32[32,8,4096]{2,1,0:T(8,128)S(1)}, f32[32,8,4096]{2,1,0:T(8,128)}, u32[]{:S(2)}) copy-start(f32[32,8,4096]{2,1,0:T(8,128)} %param.5) | copy-start | bytes 12582916
  142.1 90.6 %copy-start.4 = (f32[4,8,8,4096]{3,2,1,0:T(8,128)S(1)}, f32[4,8,8,4096]{3,2,1,0:T(8,128)}, u32[]{:S(2)}) copy-start(f32[4,8,8,4096]{3,2,1,0:T(8,128)} %reshape.469) | copy-start | bytes 12582916
  237.7 98.6 %collective-permute-start.4 = (f32[4,8,8,4096]{3,2,1,0:T(8,128)}, f32[4,8,8,4096]{3,2,1,0:T(8,128)}, u32[]{:S(2)}, u32[]{:S(2)}) collective-permute-start(f32[4,8,8,4096]{3,2,1,0:T(8,128)} %get-tuple-element.8), channel_id=1, source_target_pairs={{0,1},{1,2},{2,3},{3,4},{4,5},{5,6},{6,7},{7,8},{8,9},{9,10},{10,1... | collective-permute-start | bytes 12582920 | tf_op jit(solution)/shard_map/ppermute | solution.py:26
  244.0 182.9 %collective-permute-start.5 = (f32[4,8,8,4096]{3,2,1,0:T(8,128)}, f32[4,8,8,4096]{3,2,1,0:T(8,128)}, u32[]{:S(2)}, u32[]{:S(2)}) collective-permute-start(f32[4,8,8,4096]{3,2,1,0:T(8,128)} %get-tuple-element.7), channel_id=1, source_target_pairs={{0,2},{1,3},{2,4},{3,5},{4,6},{5,7},{6,8},{7,9},{8,10},{9,11},{10,... | collective-permute-start | bytes 12582920 | tf_op jit(solution)/shard_map/ppermute | solution.py:26
  261.7 5.0 %copy-start.7 = (f32[32,8,15,256]{3,1,2,0:T(8,128)S(1)}, f32[32,8,15,256]{3,1,2,0:T(8,128)}, u32[]{:S(2)}) copy-start(f32[32,8,15,256]{3,1,2,0:T(8,128)} %get-tuple-element.13) | copy-start | bytes 11796484
  261.7 7.7 %copy-start.6 = (f32[32,8,16,256]{3,1,2,0:T(8,128)S(1)}, f32[32,8,16,256]{3,1,2,0:T(8,128)}, u32[]{:S(2)}) copy-start(f32[32,8,16,256]{3,1,2,0:T(8,128)} %get-tuple-element.44) | copy-start | bytes 12582916
  266.7 4.1 copy-start.3
  266.7 5.3 %copy-start.5 = (f32[32,8,16,256]{3,1,2,0:T(8,128)S(1)}, f32[32,8,16,256]{3,1,2,0:T(8,128)}, u32[]{:S(2)}) copy-start(f32[32,8,16,256]{3,1,2,0:T(8,128)} %get-tuple-element.43) | copy-start | bytes 12582916
  266.7 5.3 %copy-start.8 = (f32[8]{0:T(128)S(1)}, f32[8]{0:T(128)}, u32[]{:S(2)}) copy-start(f32[8]{0:T(128)} %param.9) | copy-start | bytes 100
  266.7 5.3 %copy-start.9 = (f32[8]{0:T(128)S(1)}, f32[8]{0:T(128)}, u32[]{:S(2)}) copy-start(f32[8]{0:T(128)} %param.8) | copy-start | bytes 100
where the time goes:
time: 442 us; the launch traced here: 441 us
  waiting for transfers between devices  259 us (59%)
  local copies, waits for them, and re-layouts  78.3 us (18%)
  other arithmetic  70.3 us (16%)
  starting transfers between devices  27.3 us (6%)
  matrix products  5.35 us (1%)
    ppermute x4, waiting for transfers between devices, from_behind(): lax.ppermute(value, axis, [(source, source + steps) for source in range(f...  259 us
    ppermute x4, starting transfers between devices, from_behind(): lax.ppermute(value, axis, [(source, source + steps) for source in range(f...  17.3 us
    unnamed x23, local copies, waits for them, and re-layouts  16.4 us
    sub x1, other arithmetic, shards(): grid + diffuse * (beside_all - 6.0 * grid) - advect * (grid - behind)  12.3 us
    select_n x2, other arithmetic, gather_blocks(): departing_blocks = jnp.where(shaped, message_data, jnp.float32(0.0))  11.5 us
    concatenate x1, other arithmetic, shards(): jnp.roll(grid, extent - 1, -1)  8.99 us
    concatenate x1, other arithmetic, shards(): jnp.roll(grid, extent, -1)  8.9 us
  transfers between devices with their start and end apart: 6, of which 4 were waited for; matrix products, arithmetic and copies ran while one was open for 22% of the time, Pallas kernels for 0%

commit v1 on v0

v1 whole, which is shorter than its diff:
```python
import functools

import jax
import jax.numpy as jnp
import numpy as np
from jax import lax
from jax.experimental import pallas as pl
from jax.experimental.pallas import tpu as pltpu
from jax.sharding import PartitionSpec as P

EDGE = 16
PLANE = EDGE * EDGE
CELLS = EDGE * PLANE
FIELDS = 8
AXES = ("morton", "lane")
CAP = 3
HOLD = 4
NEAR, FAR = 2, 1
STEP = 4


def refine_tables():
    ident = np.eye(EDGE)
    slope = np.zeros((EDGE, EDGE))
    for i in range(EDGE):
        low, high = max(i - 1, 0), min(i + 1, EDGE - 1)
        slope[i, high] += 1.0 / (high - low)
        slope[i, low] -= 1.0 / (high - low)
    fine = np.stack([ident - 0.25 * slope, ident + 0.25 * slope], 1).reshape(2, EDGE, EDGE)
    crossed = np.einsum("ybj,zck->jkyzbc", fine, fine).reshape(PLANE, 4 * PLANE)
    return crossed.astype(np.float32)


def beside_table():
    turn = np.roll(np.eye(EDGE), 1, 0) + np.roll(np.eye(EDGE), -1, 0)
    return (np.kron(turn, np.eye(EDGE)) + np.kron(np.eye(EDGE), turn)).astype(np.float32)


def swaps(count):
    even = [(i, i + 1) for i in range(0, count - 1, 2)]
    odd = [(i, i + 1) for i in range(1, count - 1, 2)]
    within = [(i, i + 2) for i in range(count - 2) if i % 4 < 2]
    across = [(i, i + 2) for i in range(count - 2) if i % 4 >= 2]
    return [pairs + [(b, a) for a, b in pairs] for pairs in (even, odd, within, across)]


def exchange(parts):
    count = lax.axis_size(AXES)
    return [lax.ppermute(part, AXES, pairs) for part, pairs in zip(parts, swaps(count))]


def channel(me, offset):
    near = jnp.where((me % 2 == 0) == (offset > 0), 0, 1)
    far = jnp.where((me % 4 < 2) == (offset > 0), 2, 3)
    return jnp.where(offset == 0, -1, jnp.where(jnp.abs(offset) == 1, near, far))


def first_from(ref, total, bound):
    low = jnp.int32(0)
    for power in reversed(range(total.bit_length())):
        probe = low + (1 << power)
        below = ref[jnp.minimum(probe, total) - 1] < bound
        low = jnp.where((probe <= total) & below, probe, low)
    return low


def pack_kernel(near, far, rims, rnd_ref, flagged_ref, owner_ref, cons_ref, *refs):
    outs, sem = refs[:4], refs[4]
    own = cons_ref.shape[0]
    total = flagged_ref.shape[0]
    me = lax.axis_index(AXES)
    started = []
    if rims:
        last = cons_ref.at[own - 1, :, pl.ds(CELLS - PLANE, PLANE)]
        first = cons_ref.at[0, :, pl.ds(0, PLANE)]
        for place, front, out in ((0, me % 2 == 0, outs[0]), (1, me % 2 == 1, outs[1])):
            target = out.at[:, pl.ds(near * CELLS, PLANE)]

            @pl.when(front)
            def _():
                pltpu.make_async_copy(last, target, sem.at[HOLD + place]).start()

            @pl.when(jnp.logical_not(front))
            def _():
                pltpu.make_async_copy(first, target, sem.at[HOLD + place]).start()

    start = first_from(flagged_ref, total, me * own)
    offsets = []
    for k in range(HOLD):
        place = jnp.minimum(start + k, total - 1)
        block = flagged_ref[place] - me * own
        mine = (start + k < total) & (block < own)
        block = jnp.clip(block, 0, own - 1)
        offset = owner_ref[place] - me
        offset = jnp.where(mine, offset, 0)
        rank = sum(((o == offset).astype(jnp.int32) for o in offsets), jnp.int32(0))
        offsets.append(jnp.where(mine, offset, 99))
        way = channel(me, offset)
        slot = rank - jnp.where(way < 2, rnd_ref[0], rnd_ref[1])
        fits = (way >= 0) & (slot >= 0) & (slot < jnp.where(way < 2, near, far))
        started.append(fits)
        for c, out in enumerate(outs):
            slots = near if c < 2 else far

            @pl.when(fits & (way == c))
            def _(c=c, out=out, slots=slots):
                column = pl.multiple_of(jnp.clip(slot, 0, slots - 1) * CELLS, CELLS)
                pltpu.make_async_copy(cons_ref.at[block], out.at[:, pl.ds(column, CELLS)], sem.at[k]).start()

    for k, fits in enumerate(started):

        @pl.when(fits)
        def _(k=k):
            pltpu.make_async_copy(cons_ref.at[0], outs[2].at[:, pl.ds(0, CELLS)], sem.at[k]).wait()

    if rims:
        for place in range(2):
            target = outs[place].at[:, pl.ds(near * CELLS, PLANE)]
            pltpu.make_async_copy(cons_ref.at[0, :, pl.ds(0, PLANE)], target, sem.at[HOLD + place]).wait()


def pack(rnd, flagged, owner, cons, near, far, rims):
    fields = cons.shape[1]
    wide = near * CELLS + (PLANE if rims else 0)
    shapes = [jax.ShapeDtypeStruct((fields, width), jnp.float32) for width in (wide, wide, far * CELLS, far * CELLS)]
    smem = pl.BlockSpec(memory_space=pltpu.SMEM)
    anywhere = pl.BlockSpec(memory_space=pl.ANY)
    return pl.pallas_call(
        functools.partial(pack_kernel, near, far, rims),
        out_shape=shapes,
        in_specs=[smem, smem, smem, anywhere],
        out_specs=[anywhere] * 4,
        scratch_shapes=[pltpu.SemaphoreType.DMA((HOLD + 2,))],
        cost_estimate=pl.CostEstimate(flops=0, bytes_accessed=1 << 20, transcendentals=0),
        name="pack",
    )(rnd, flagged, owner, cons)


def by_field(ref, fields):
    rows = lax.broadcasted_iota(jnp.int32, (fields, PLANE), 0)
    value = jnp.zeros((fields, PLANE), jnp.float32)
    for f in range(fields):
        value = jnp.where(rows == f, ref[f], value)
    return value


def split(value):
    high = value.astype(jnp.bfloat16)
    return high, (value - high.astype(jnp.float32)).astype(jnp.bfloat16)


def dot_split(value, table):
    return sum(jnp.dot(part, table, preferred_element_type=jnp.float32) for part in split(value))


def planes_of(block):
    return [block[:, x * PLANE : (x + 1) * PLANE] for x in range(EDGE)]


def coarse_kernel(diff_ref, cour_ref, block_ref, before_ref, after_ref, table_ref, out_ref, edge_ref):
    step = pl.program_id(0)
    steps = pl.num_programs(0)
    count, fields, _ = block_ref.shape
    diffuse = by_field(diff_ref, fields)
    courant = by_field(cour_ref, fields)
    centre = 1.0 - 6.0 * diffuse - courant
    back = diffuse + courant
    table = table_ref[...].astype(jnp.bfloat16)
    for b in range(count):
        planes = planes_of(block_ref[b])
        beside = dot_split(jnp.concatenate(planes, 0), table)
        if b > 0:
            low = block_ref[b - 1, :, pl.ds(CELLS - PLANE, PLANE)]
        else:
            low = jnp.where(step > 0, before_ref[0], 0.0)
        if b < count - 1:
            high = block_ref[b + 1, :, pl.ds(0, PLANE)]
        else:
            high = jnp.where(step < steps - 1, after_ref[0], 0.0)
        padded = [low] + planes + [high]
        for x in range(EDGE):
            ring = beside[x * fields : (x + 1) * fields]
            stepped = centre * padded[x + 1] + back * padded[x] + diffuse * (padded[x + 2] + ring)
            out_ref[b, :, pl.ds(x * PLANE, PLANE)] = stepped
            if b == 0 and x == 0:

                @pl.when(step == 0)
                def _():
                    edge_ref[0] = stepped

            if b == count - 1 and x == EDGE - 1:

                @pl.when(step == steps - 1)
                def _():
                    edge_ref[1] = stepped


def coarse(diffusivity, courant, cons):
    own, fields, cells = cons.shape
    smem = pl.BlockSpec(memory_space=pltpu.SMEM)
    return pl.pallas_call(
        coarse_kernel,
        grid=(own // STEP,),
        out_shape=[
            jax.ShapeDtypeStruct(cons.shape, jnp.float32),
            jax.ShapeDtypeStruct((2, fields, PLANE), jnp.float32),
        ],
        in_specs=[
            smem,
            smem,
            pl.BlockSpec((STEP, fields, cells), lambda i: (i, 0, 0)),
            pl.BlockSpec((1, fields, PLANE), lambda i: (jnp.maximum(i * STEP - 1, 0), 0, EDGE - 1)),
            pl.BlockSpec((1, fields, PLANE), lambda i: (jnp.minimum((i + 1) * STEP, own - 1), 0, 0)),
            pl.BlockSpec((PLANE, PLANE), lambda i: (0, 0)),
        ],
        out_specs=[
            pl.BlockSpec((STEP, fields, cells), lambda i: (i, 0, 0)),
            pl.BlockSpec((2, fields, PLANE), lambda i: (0, 0, 0)),
        ],
        compiler_params=pltpu.CompilerParams(vmem_limit_bytes=32 << 20),
        cost_estimate=pl.CostEstimate(flops=2 * 2 * own * EDGE * fields * PLANE * PLANE, bytes_accessed=8 << 20, transcendentals=0),
        name="coarse",
    )(diffusivity, courant, cons, cons, cons, jnp.asarray(beside_table()))


def refine(parent, table, out_ref):
    fields = parent.shape[0]
    fine = dot_split(jnp.concatenate(planes_of(parent), 0), table)
    rows = [fine[x * fields : (x + 1) * fields] for x in range(EDGE)]
    for x in range(EDGE):
        low, high = max(x - 1, 0), min(x + 1, EDGE - 1)
        slope = (rows[high] - rows[low]) * (0.25 / (high - low))
        half, place = divmod(2 * x, EDGE)
        for odd, value in enumerate((rows[x] - slope, rows[x] + slope)):
            for q in range(4):
                out_ref[half * 4 + q, :, pl.ds((place + odd) * PLANE, PLANE)] = value[:, q * PLANE : (q + 1) * PLANE]


def unpack_kernel(near, far, rims, *refs):
    if rims:
        rnd_ref, flagged_ref, owner_ref, diff_ref, cour_ref, cons_ref, *refs = refs
        parts, (edge_ref, table_ref, _, coarse_ref, children_ref), refs = refs[:4], refs[4:9], refs[9:]
        parent_ref, child_ref, rim_ref, sem = refs
    else:
        rnd_ref, flagged_ref, owner_ref, cons_ref, *refs = refs
        parts, (table_ref, _, children_ref), refs = refs[:4], refs[4:7], refs[7:]
        parent_ref, child_ref, sem = refs
    own = cons_ref.shape[0]
    total = flagged_ref.shape[0]
    me = lax.axis_index(AXES)
    start = first_from(owner_ref, total, me)
    offsets, loads, stores = [], [], []
    for s in range(CAP):
        place = jnp.minimum(start + s, total - 1)
        mine = (start + s < total) & (owner_ref[place] == me)
        block = flagged_ref[place]
        source = block // own
        offset = source - me
        rank = sum(((o == offset).astype(jnp.int32) for o in offsets), jnp.int32(0))
        offsets.append(jnp.where(mine, offset, 99))
        way = channel(me, offset)
        slot = rank - jnp.where(way < 2, rnd_ref[0], rnd_ref[1])
        fits = (slot >= 0) & (slot < jnp.where(way < 2, near, far))
        here = way < 0
        load = mine & (jnp.logical_not(here) & fits | here) if rims else mine & jnp.logical_not(here) & fits
        loads.append(load)
        stores.append(load | jnp.logical_not(mine) if rims else load)
        if rims:

            @pl.when(load & here)
            def _():
                local = jnp.clip(block - me * own, 0, own - 1)
                pltpu.make_async_copy(cons_ref.at[local], parent_ref.at[s], sem.at[s]).start()

        for c, part in enumerate(parts):
            slots = near if c < 2 else far

            @pl.when(load & (way == c))
            def _(c=c, part=part, slots=slots):
                column = pl.multiple_of(jnp.clip(slot, 0, slots - 1) * CELLS, CELLS)
                pltpu.make_async_copy(part.at[:, pl.ds(column, CELLS)], parent_ref.at[s], sem.at[s]).start()

    if rims:
        fields = cons_ref.shape[1]
        rim_at = pl.ds(near * CELLS, PLANE)
        fetch = [pltpu.make_async_copy(parts[c].at[:, rim_at], rim_ref.at[c], sem.at[2 * CAP + c]) for c in range(2)]
        for copy in fetch:
            copy.start()
        for copy in fetch:
            copy.wait()
        diffuse = by_field(diff_ref, fields)
        courant = by_field(cour_ref, fields)
        odd = me % 2 == 1
        low = jnp.where(odd, rim_ref[0], rim_ref[1])
        high = jnp.where(odd, rim_ref[1], rim_ref[0])
        rim_ref[2] = edge_ref[0] + (diffuse + courant) * low
        rim_ref[3] = edge_ref[1] + diffuse * high
        spots = (coarse_ref.at[0, :, pl.ds(0, PLANE)], coarse_ref.at[own - 1, :, pl.ds(CELLS - PLANE, PLANE)])
        ends = [pltpu.make_async_copy(rim_ref.at[2 + c], spots[c], sem.at[2 * CAP + 2 + c]) for c in range(2)]
        for copy in ends:
            copy.start()

    table = table_ref[...].astype(jnp.bfloat16)
    for s in range(CAP):

        @pl.when(loads[s])
        def _(s=s):
            pltpu.make_async_copy(cons_ref.at[0], parent_ref.at[s], sem.at[s]).wait()
            refine(parent_ref[s], table, child_ref.at[s])

        if rims:

            @pl.when(stores[s] & jnp.logical_not(loads[s]))
            def _(s=s):
                child_ref[s] = jnp.zeros(child_ref.shape[1:], jnp.float32)

        @pl.when(stores[s])
        def _(s=s):
            pltpu.make_async_copy(child_ref.at[s], children_ref.at[s], sem.at[CAP + s]).start()

    for s in range(CAP):

        @pl.when(stores[s])
        def _(s=s):
            pltpu.make_async_copy(child_ref.at[s], children_ref.at[s], sem.at[CAP + s]).wait()

    if rims:
        for copy in ends:
            copy.wait()


def unpack(rnd, flagged, owner, cons, parts, near, far, final=None, children=None):
    fields = cons.shape[1]
    smem = pl.BlockSpec(memory_space=pltpu.SMEM)
    vmem = pl.BlockSpec(memory_space=pltpu.VMEM)
    anywhere = pl.BlockSpec(memory_space=pl.ANY)
    hbm = pl.BlockSpec(memory_space=pltpu.HBM)
    family = jax.ShapeDtypeStruct((CAP, 8, fields, CELLS), jnp.float32)
    table = jnp.asarray(refine_tables())
    rims = final is not None
    scratch = [pltpu.VMEM((CAP, fields, CELLS), jnp.float32), pltpu.VMEM(family.shape, jnp.float32)]
    params = dict(
        compiler_params=pltpu.CompilerParams(vmem_limit_bytes=32 << 20),
        cost_estimate=pl.CostEstimate(flops=2 * 2 * CAP * EDGE * fields * PLANE * 4 * PLANE, bytes_accessed=5 << 20, transcendentals=0),
        name="unpack",
    )
    kernel = functools.partial(unpack_kernel, near, far, rims)
    if rims:
        diffusivity, courant, stepped, edges = final
        return pl.pallas_call(
            kernel,
            out_shape=[jax.ShapeDtypeStruct(stepped.shape, jnp.float32), family],
            in_specs=[smem] * 5 + [anywhere] * 5 + [vmem, vmem, hbm],
            out_specs=[hbm, hbm],
            scratch_shapes=scratch + [pltpu.VMEM((4, fields, PLANE), jnp.float32), pltpu.SemaphoreType.DMA((2 * CAP + 4,))],
            input_output_aliases={12: 0},
            **params,
        )(rnd, flagged, owner, diffusivity, courant, cons, *parts, edges, table, stepped)
    return pl.pallas_call(
        kernel,
        out_shape=family,
        in_specs=[smem] * 3 + [anywhere] * 5 + [vmem, hbm],
        out_specs=hbm,
        scratch_shapes=scratch + [pltpu.SemaphoreType.DMA((2 * CAP,))],
        input_output_aliases={9: 0},
        **params,
    )(rnd, flagged, owner, cons, *parts, table, children)


def rounds_left(flagged, owner, own):
    source = flagged // own
    offset = owner - source
    near, far = jnp.abs(offset) == 1, jnp.abs(offset) == 2
    key = source * 8 + offset
    left = jnp.int32(0)
    more = [jnp.any(kind[k:] & (key[k:] == key[:-k])) for kind, k in ((near, NEAR), (far, FAR), (far, FAR + 1))]
    near3, far2, far3 = (flag.astype(jnp.int32) for flag in more)
    return jnp.maximum(near3, far2 + far3)


def shards(cons_old, flagged, new_owner, diffusivity, courant):
    zero = jnp.zeros((2,), jnp.int32)
    parts = pack(zero, flagged, new_owner, cons_old, NEAR, FAR, True)
    arrived = exchange(parts)
    stepped, edges = coarse(diffusivity, courant, cons_old)
    final = (diffusivity, courant, stepped, edges)
    coarse_next, children = unpack(zero, flagged, new_owner, cons_old, arrived, NEAR, FAR, final)
    left = rounds_left(flagged, new_owner, cons_old.shape[0])

    def later(carry):
        turn, children = carry
        base = jnp.stack([NEAR + turn, FAR + turn]).astype(jnp.int32)
        parts = pack(base, flagged, new_owner, cons_old, 1, 1, False)
        children = unpack(base, flagged, new_owner, cons_old, exchange(parts), 1, 1, children=children)
        return turn + 1, children

    _, children = lax.while_loop(lambda carry: carry[0] < left, later, (jnp.int32(0), children))
    return coarse_next, children


def solution(mesh):
    in_specs = (P(AXES, None, None), P(), P(), P(), P())
    out_specs = (P(AXES, None, None), P(AXES, None, None, None))
    return jax.shard_map(shards, mesh=mesh, in_specs=in_specs, out_specs=out_specs, check_vma=False)
```

time: 442 us -> 42.6 us (0.10)
  the two profiles are of different devices: /device:TPU:96 before, /device:TPU:32 now
where the time goes in v1:
time: 42.6 us; the launch traced here: 42.9 us
  starting transfers between devices  23.6 us (55%)
  Pallas kernels  14.5 us (34%)
  between operations  2.67 us (6%)
  other arithmetic  1.46 us (3%)
  local copies, waits for them, and re-layouts  0.62 us (1%)
    ppermute x4, starting transfers between devices, exchange(): lax.ppermute(part, AXES, pairs)  23.6 us
    pallas_call x1, Pallas kernels, coarse(): pl.pallas_call(coarse_kernel, grid=(own // STEP,), out_shape=[jax.ShapeDt...  8.76 us
    pallas_call x1, Pallas kernels, unpack(): pl.pallas_call(kernel, out_shape=[jax.ShapeDtypeStruct(stepped.shape, jnp...  3.34 us
    pallas_call x1, Pallas kernels, pack(): pl.pallas_call(functools.partial(pack_kernel, near, far, rims), out_shape...  2.38 us
    reduce_or x2, other arithmetic, rounds_left(): jnp.any(kind[k:] & (key[k:] == key[:-k]))  1.43 us
  transfers between devices with their start and end apart: 4, of which 0 were waited for; matrix products, arithmetic and copies ran while one was open for 3% of the time, Pallas kernels for 20%

profile of v1, /device:TPU:32, one launch (start us, length us, event | category | flops | bytes accessed | tf_op | source)
XLA Modules:
  0.0 42.9 jit_solution(9958356769343553944)
XLA Ops:
  0.6 0.0 copy-start
  0.6 0.0 copy-start.8
  0.7 0.0 copy-start.7
  0.7 0.0 copy-start.2
  0.7 0.0 copy-start.3
  0.7 0.6 %broadcast_1_rnd_ref_refs_0_.2.rnd_ref.refs_0_ = s32[2]{0:T(128)} broadcast(s32[]{:T(128)} %copy.21), dimensions={} | broadcast | bytes 12 | tf_op jit(solution)/shard_map/broadcast.1.rnd_ref.refs_0_
  1.3 2.4 %pack.2 = (f32[8,8448]{1,0:T(8,128)}, f32[8,8448]{1,0:T(8,128)}, f32[8,4096]{1,0:T(8,128)}, f32[8,4096]{1,0:T(8,128)}) custom-call(s32[2]{0:T(128)} %broadcast_1_rnd_ref_refs_0_.2.rnd_ref.refs_0_, s32[256]{0:T(256)} %refs_1_.1, s32[256]{0:T(256)} %refs_2_.1, f32[32,8,4096]{2,1,0:T(8,128)} %refs_5_.1), custom_call_target="tpu_custom_call" | custom-call | bytes 1048576 | tf_op jit(solution)/shard_map/pack/pallas_call | solution.py:128
  3.6 5.5 %collective-permute-start.4 = (f32[8,8448]{1,0:T(8,128)}, f32[8,8448]{1,0:T(8,128)S(1)}, u32[]{:S(2)}, u32[]{:S(2)}) collective-permute-start(f32[8,8448]{1,0:T(8,128)} %get-tuple-element.52), channel_id=1, source_target_pairs={{0,1},{2,3},{4,5},{6,7},{8,9},{10,11},{12,13},{14,15},{16,17},{18,... | collective-permute-start | bytes 811016 | tf_op jit(solution)/shard_map/ppermute | solution.py:49
  9.2 9.1 %collective-permute-start.5 = (f32[8,8448]{1,0:T(8,128)}, f32[8,8448]{1,0:T(8,128)S(1)}, u32[]{:S(2)}, u32[]{:S(2)}) collective-permute-start(f32[8,8448]{1,0:T(8,128)} %get-tuple-element.53), channel_id=1, source_target_pairs={{1,2},{3,4},{5,6},{7,8},{9,10},{11,12},{13,14},{15,16},{17,18},{19... | collective-permute-start | bytes 811016 | tf_op jit(solution)/shard_map/ppermute | solution.py:49
  18.3 0.1 collective-permute-start.6
  18.4 8.9 %collective-permute-start.7 = (f32[8,4096]{1,0:T(8,128)}, f32[8,4096]{1,0:T(8,128)S(1)}, u32[]{:S(2)}, u32[]{:S(2)}) collective-permute-start(f32[8,4096]{1,0:T(8,128)} %get-tuple-element.55), channel_id=1, source_target_pairs={{2,4},{3,5},{6,8},{7,9},{10,12},{11,13},{14,16},{15,17},{18,20},{1... | collective-permute-start | bytes 393224 | tf_op jit(solution)/shard_map/ppermute | solution.py:49
  27.3 0.0 copy-done.8
  27.3 0.0 copy-done.7
  27.3 0.7 %and_reduce_fusion = (pred[]{:T(512)}, pred[]{:T(512)}) fusion(pred[256]{0:T(512)(128)(4,1)S(1)} %abs_compare_fusion, pred[256]{0:T(512)(128)(4,1)S(1)} %get-tuple-element.105, s32[256]{0:T(256)S(1)} %multiply_add_fusion), kind=kLoop, calls=%fused_computation.1 | loop fusion | flops 1268 | bytes 2542 | tf_op jit(solution)/shard_map/reduce_or | solution.py:376
  28.1 0.7 %and_reduce_fusion.1 = pred[]{:T(512)} fusion(pred[256]{0:T(512)(128)(4,1)S(1)} %abs_compare_fusion, s32[256]{0:T(256)S(1)} %multiply_add_fusion), kind=kLoop, calls=%fused_computation.2 | loop fusion | flops 764 | bytes 2296 | tf_op jit(solution)/shard_map/reduce_or | solution.py:376
  30.6 0.0 copy-done
  30.6 0.0 copy-done.2
  30.6 0.0 copy-done.3
  30.6 0.0 copy-start.4
  30.7 0.0 copy-start.5
  30.7 0.0 copy-start.6
  30.7 8.8 %coarse.1 = (f32[32,8,4096]{2,1,0:T(8,128)}, f32[2,8,256]{2,1,0:T(8,128)S(1)}) custom-call(f32[8]{0:T(128)S(1)} %copy-done.2, f32[8]{0:T(128)S(1)} %copy-done.3, f32[32,8,4096]{2,1,0:T(8,128)} %refs_5_.1, f32[32,8,4096]{2,1,0:T(8,128)} %refs_5_.1, f32[32,8,4096]{2,1,0:T(8,128)} %refs_5_.1, f32[256,256]{1,0:T(8,128)S(1)} %copy-done), custom_call_target="tpu_custom_call" | custom-call | flops 1073741824 | bytes 8388608 | tf_op jit(solution)/shard_map/coarse/pallas_call | solution.py:201
  39.4 0.0 collective-permute-done.6.refs_8_
  39.4 0.0 collective-permute-done.7.refs_9_
  39.4 0.0 collective-permute-done.4.refs_6_
  39.5 0.0 collective-permute-done.5.refs_7_
  39.5 0.0 copy-done.4
  39.5 0.0 copy-done.5
  39.5 0.0 copy-done.6
  39.5 3.3 %unpack.2 = (f32[32,8,4096]{2,1,0:T(8,128)}, f32[3,8,8,4096]{3,2,1,0:T(8,128)}) custom-call(s32[2]{0:T(128)S(1)} %copy-done.4, s32[256]{0:T(256)S(1)} %copy-done.8, s32[256]{0:T(256)S(1)} %copy-done.7, f32[8]{0:T(128)S(1)} %copy-done.2, f32[8]{0:T(128)S(1)} %copy-done.3, f32[32,8,4096]{2,1,0:T(8,128)S(1)} %copy-done.5, ...), custom_call_target="tpu_custom_call", output_to_operand_aliasing={{0}: (12, {})} | custom-call | flops 402653184 | bytes 5242880 | tf_op jit(solution)/shard_map/unpack/pallas_call | solution.py:350
  (4 shorter events, 0.0 us)
Async XLA Ops:
  0.6 30.0 %copy-start = (f32[256,256]{1,0:T(8,128)S(1)}, f32[256,256]{1,0:T(8,128)}, u32[]{:S(2)}) copy-start(f32[256,256]{1,0:T(8,128)} %constant.33.clone.table_ref) | copy-start | bytes 786436
  0.6 26.6 %copy-start.8 = (s32[256]{0:T(256)S(1)}, s32[256]{0:T(256)}, u32[]{:S(2)}) copy-start(s32[256]{0:T(256)} %refs_1_.1) | copy-start | bytes 3076
  0.7 26.6 %copy-start.7 = (s32[256]{0:T(256)S(1)}, s32[256]{0:T(256)}, u32[]{:S(2)}) copy-start(s32[256]{0:T(256)} %refs_2_.1) | copy-start | bytes 3076
  0.7 30.0 %copy-start.2 = (f32[8]{0:T(128)S(1)}, f32[8]{0:T(128)}, u32[]{:S(2)}) copy-start(f32[8]{0:T(128)} %refs_3_.1) | copy-start | bytes 100
  0.7 30.0 %copy-start.3 = (f32[8]{0:T(128)S(1)}, f32[8]{0:T(128)}, u32[]{:S(2)}) copy-start(f32[8]{0:T(128)} %refs_4_.1) | copy-start | bytes 100
  3.6 35.8 %collective-permute-start.4 = (f32[8,8448]{1,0:T(8,128)}, f32[8,8448]{1,0:T(8,128)S(1)}, u32[]{:S(2)}, u32[]{:S(2)}) collective-permute-start(f32[8,8448]{1,0:T(8,128)} %get-tuple-element.52), channel_id=1, source_target_pairs={{0,1},{2,3},{4,5},{6,7},{8,9},{10,11},{12,13},{14,15},{16,17},{18,... | collective-permute-start | bytes 811016 | tf_op jit(solution)/shard_map/ppermute | solution.py:49
  9.2 30.3 %collective-permute-start.5 = (f32[8,8448]{1,0:T(8,128)}, f32[8,8448]{1,0:T(8,128)S(1)}, u32[]{:S(2)}, u32[]{:S(2)}) collective-permute-start(f32[8,8448]{1,0:T(8,128)} %get-tuple-element.53), channel_id=1, source_target_pairs={{1,2},{3,4},{5,6},{7,8},{9,10},{11,12},{13,14},{15,16},{17,18},{19... | collective-permute-start | bytes 811016 | tf_op jit(solution)/shard_map/ppermute | solution.py:49
  18.3 21.1 %collective-permute-start.6 = (f32[8,4096]{1,0:T(8,128)}, f32[8,4096]{1,0:T(8,128)S(1)}, u32[]{:S(2)}, u32[]{:S(2)}) collective-permute-start(f32[8,4096]{1,0:T(8,128)} %get-tuple-element.54), channel_id=1, source_target_pairs={{0,2},{1,3},{4,6},{5,7},{8,10},{9,11},{12,14},{13,15},{16,18},{17,... | collective-permute-start | bytes 393224 | tf_op jit(solution)/shard_map/ppermute | solution.py:49
  18.4 21.0 %collective-permute-start.7 = (f32[8,4096]{1,0:T(8,128)}, f32[8,4096]{1,0:T(8,128)S(1)}, u32[]{:S(2)}, u32[]{:S(2)}) collective-permute-start(f32[8,4096]{1,0:T(8,128)} %get-tuple-element.55), channel_id=1, source_target_pairs={{2,4},{3,5},{6,8},{7,9},{10,12},{11,13},{14,16},{15,17},{18,20},{1... | collective-permute-start | bytes 393224 | tf_op jit(solution)/shard_map/ppermute | solution.py:49
  30.6 8.8 %copy-start.4 = (s32[2]{0:T(128)S(1)}, s32[2]{0:T(128)}, u32[]{:S(2)}) copy-start(s32[2]{0:T(128)} %broadcast_1_rnd_ref_refs_0_.2.rnd_ref.refs_0_) | copy-start | bytes 28
  30.7 8.8 %copy-start.5 = (f32[32,8,4096]{2,1,0:T(8,128)S(1)}, f32[32,8,4096]{2,1,0:T(8,128)}, u32[]{:S(2)}) copy-start(f32[32,8,4096]{2,1,0:T(8,128)} %refs_5_.1) | copy-start | bytes 12582916
  30.7 8.8 %copy-start.6 = (f32[256,1024]{1,0:T(8,128)S(1)}, f32[256,1024]{1,0:T(8,128)}, u32[]{:S(2)}) copy-start(f32[256,1024]{1,0:T(8,128)} %constant.34.clone.refs_11_) | copy-start | bytes 3145732
